TPU v7x, 256 devices: a whole 4x4x8 slice. The times are simulated.
256 devices in a mesh: sx: 8 (over z), sy: 8 (over y, core), batch: 4 (over x).
Axes of the slice: x: 4, y: 4, z: 8, core: 2. Of those that a mesh axis runs over, the one named last changes fastest.
Arguments:
- volume: bfloat16 [4, 64, 32, 128, 128], P('batch', None, 'sx', 'sy'), may hold values from -40 to 40
- conv_weight: bfloat16 [64, 64, 3, 3, 3], replicated, may hold values from -0.15625 to 0.15625
- out_gain: float32 [64], replicated, may hold values from 0.5 to 1.5
- out_shift: float32 [64], replicated, may hold values from -3 to 3
Outputs:
- whitened: float32 [4, 64, 32, 128, 128], P('batch', None, 'sx', 'sy')
All inputs are finite; a program needn't handle non-finite values.
Results may differ from a plain program's by a relative error of at most 0.0007.
Values may be sent and summed in bfloat16 or wider, within the bound.
A program may use at most 64 MiB of HBM per device.

v0:
```python
import jax
import jax.numpy as jnp
from jax import lax
from jax.sharding import PartitionSpec as P

NS_ITERS = 5


def extended_2(cells, sides, width):
    for axis, dim in sides:
        count = lax.axis_size(axis)
        ends = count - 1
        head = lax.slice_in_dim(cells, 0, width, axis=dim)
        tail = lax.slice_in_dim(cells, cells.shape[dim] - width, cells.shape[dim], axis=dim)
        cells = jnp.concatenate(
            [
                lax.ppermute(tail, axis, [(i, (i + 1) % count) for i in range(ends)]),
                cells,
                lax.ppermute(head, axis, [((i + 1) % count, i) for i in range(ends)]),
            ],
            axis=dim,
        )
    return cells


def on_device(volume, conv_weight, out_gain, out_shift):
    extended = extended_2(volume, (("sx", 2), ("sy", 3)), 1)
    response = lax.conv_general_dilated(
        extended,
        conv_weight,
        (1, 1, 1),
        [(0, 0), (0, 0), (1, 1)],
        dimension_numbers=("NCDHW", "OIDHW", "NCDHW"),
        preferred_element_type=jnp.float32,
    )
    samples = response.shape[0]
    channels = response.shape[1]
    flat = response.reshape(samples, channels, -1)
    local_count = samples * flat.shape[2]
    total_count = float(
        local_count * lax.axis_size("sx") * lax.axis_size("sy") * lax.axis_size("batch")
    )
    local_sum = jnp.sum(flat, axis=(0, 2))
    highest = lax.Precision.HIGHEST
    channel_mean = lax.psum(local_sum, ("sx", "sy", "batch")) / total_count
    centered = flat - channel_mean[None, :, None]
    products = jnp.einsum("scn,sdn->cd", centered, centered, precision=highest)
    covariance = lax.psum(products, ("sx", "sy", "batch")) / total_count
    sigma = covariance + 1e-05 * jnp.eye(channels, dtype=jnp.float32)
    trace_total = jnp.trace(sigma)
    normed = sigma / trace_total
    factor = jnp.eye(channels, dtype=jnp.float32)
    for turn in range(NS_ITERS):
        cubed = jnp.dot(jnp.dot(factor, factor, precision=highest), factor, precision=highest)
        factor = 1.5 * factor - 0.5 * jnp.dot(cubed, normed, precision=highest)
    whiten = factor / jnp.sqrt(trace_total)
    mixed = jnp.einsum("cd,sdn->scn", whiten, centered, precision=highest)
    result = out_gain[None, :, None] * mixed + out_shift[None, :, None]
    return result.reshape(response.shape)


def solution(mesh):
    in_specs = (P("batch", None, "sx", "sy", None), P(), P(), P())
    out_specs = P("batch", None, "sx", "sy", None)
    return jax.shard_map(
        on_device, mesh=mesh, in_specs=in_specs, out_specs=out_specs, check_vma=False
    )
```

profile of v0, /device:TPU:1, one launch (start us, length us, event | category | flops | bytes accessed | tf_op | source)
XLA Modules:
  0.0 251.8 jit_solution(2928528203032463123)
XLA Ops:
  0.0 0.0 copy-start
  0.0 0.0 copy-start.2
  0.0 1.2 fusion.41
  1.2 0.1 copy.33
  1.3 4.4 %collective-permute-start = (bf16[1,64,1,16,128]{4,1,3,2,0:T(8,128)(2,1)S(1)}, bf16[1,64,1,16,128]{4,1,3,2,0:T(8,128)(2,1)S(1)}, u32[]{:S(2)}, u32[]{:S(2)}) collective-permute-start(bf16[1,64,1,16,128]{4,1,3,2,0:T(8,128)(2,1)S(1)} %copy.33), channel_id=1, source_target_pairs={{0,32},{32,64},{64,96},{96,128},{128,160},{160,192},{192,224},{1,3... | collective-permute-start | bytes 786440 | tf_op jit(solution)/shard_map/ppermute | solution.py:17
  5.7 0.1 copy.34
  5.7 1.3 collective-permute-start.1
  7.0 0.1 fusion.30
  7.2 3.4 %collective-permute-done = bf16[1,64,1,16,128]{4,1,3,2,0:T(8,128)(2,1)S(1)} collective-permute-done((bf16[1,64,1,16,128]{4,1,3,2,0:T(8,128)(2,1)S(1)}, bf16[1,64,1,16,128]{4,1,3,2,0:T(8,128)(2,1)S(1)}, u32[]{:S(2)}, u32[]{:S(2)}) %collective-permute-start) | collective-permute-done | bytes 262176 | tf_op jit(solution)/shard_map/ppermute | solution.py:17
  10.6 0.0 copy-done.2
  10.6 0.7 constant_dynamic-update-slice_fusion.1
  11.4 3.5 %collective-permute-done.1 = bf16[1,64,1,16,128]{4,1,3,2,0:T(8,128)(2,1)S(1)} collective-permute-done((bf16[1,64,1,16,128]{4,1,3,2,0:T(8,128)(2,1)S(1)}, bf16[1,64,1,16,128]{4,1,3,2,0:T(8,128)(2,1)S(1)}, u32[]{:S(2)}, u32[]{:S(2)}) %collective-permute-start.1) | collective-permute-done | bytes 262176 | tf_op jit(solution)/shard_map/ppermute | solution.py:19
  14.9 4.8 %collective-permute-start.2 = (bf16[1,64,6,1,128]{4,1,3,2,0:T(8,128)(2,1)S(1)}, bf16[1,64,6,1,128]{4,1,3,2,0:T(8,128)(2,1)S(1)}, u32[]{:S(2)}, u32[]{:S(2)}) collective-permute-start(bf16[1,64,6,1,128]{4,1,3,2,0:T(8,128)(2,1)S(1)} %get-tuple-element.5), channel_id=1, source_target_pairs={{0,4},{4,8},{8,12},{12,16},{16,20},{20,24},{24,28},{1,5},{5,9},{9,... | collective-permute-start | bytes 294920 | tf_op jit(solution)/shard_map/ppermute | solution.py:17
  19.7 1.9 collective-permute-start.3
  21.6 0.1 fusion.29
  21.8 0.0 collective-permute-done.2
  21.8 3.8 %collective-permute-done.3 = bf16[1,64,6,1,128]{4,1,3,2,0:T(8,128)(2,1)S(1)} collective-permute-done((bf16[1,64,6,1,128]{4,1,3,2,0:T(8,128)(2,1)S(1)}, bf16[1,64,6,1,128]{4,1,3,2,0:T(8,128)(2,1)S(1)}, u32[]{:S(2)}, u32[]{:S(2)}) %collective-permute-start.3) | collective-permute-done | bytes 98336 | tf_op jit(solution)/shard_map/ppermute | solution.py:19
  25.6 0.2 maximum_bitcast_fusion
  25.9 2.9 %copy.30 = bf16[64,6,18,1,128]{0,4,2,1,3:T(8,128)(2,1)} copy(bf16[64,6,18,1,128]{4,0,2,1,3:T(8,128)(2,1)S(1)} %maximum_bitcast_fusion) | data formatting | bytes 3538944
  28.8 5.4 %pad.clone = bf16[64,6,18,1,136]{0,4,2,1,3:T(8,128)(2,1)} pad(bf16[64,6,18,1,128]{0,4,2,1,3:T(8,128)(2,1)} %copy.30, bf16[]{:T(256)} %constant.20), padding=0_0x0_0x0_0x0_0x1_7 | pad | bytes 3649538 | tf_op jit(solution)/shard_map/concatenate | solution.py:15
  34.2 7.7 %reshape.53 = bf16[64,6,18,1,8,17]{0,5,4,2,1,3:T(8,128)(2,1)} reshape(bf16[64,6,18,1,136]{0,4,2,1,3:T(8,128)(2,1)} %pad.clone) | data formatting | bytes 3760128 | tf_op jit(solution)/shard_map/conv_general_dilated | solution.py:28
  42.0 0.0 copy-start.5
  42.0 3.2 %copy.23 = bf16[64,6,18,1,8,17]{0,4,5,2,1,3:T(8,128)(2,1)S(1)} copy(bf16[64,6,18,1,8,17]{0,5,4,2,1,3:T(8,128)(2,1)} %reshape.53) | data formatting | bytes 3760128 | tf_op jit(solution)/shard_map/conv_general_dilated | solution.py:28
  45.2 0.1 slice.23
  45.3 0.0 copy-done
  45.3 0.0 copy-done.5
  45.3 18.2 %select_reduce_fusion = (f32[64]{0:T(128)S(1)}, f32[4,16,8,17,64]{4,2,3,1,0:T(8,128)}) fusion(pred[8,17]{0,1:T(8,128)(4,1)S(1)} %copy-done.5, bf16[64,64,3,3,3]{1,0,4,3,2:T(8,128)(2,1)S(1)} %copy-done, bf16[64,6,18,1,7,2]{0,4,5,2,1,3:T(8,128)(2,1)S(1)} %slice.23, bf16[64,6,18,1,8,17]{0,4,5,2,1,3:T(8,128)(2,1)S(1)} %copy.23), kind=kOutput, calls=%fused_computation.5 | convolution fusion | flops 1933160448 | bytes 4523400 | tf_op jit(solution)/shard_map/conv_general_dilated | solution.py:28
  63.6 79.4 %psum.14 = f32[64]{0:T(128)S(1)} all-reduce(f32[64]{0:T(128)S(1)} %get-tuple-element.9), channel_id=1, replica_groups=mesh['sx'=8,'sy'=8,'batch'=4] {'sx','sy','batch'}, use_global_device_ids=true, to_apply=%region_1.0 | all-reduce | flops 64 | bytes 512 | tf_op jit(solution)/shard_map/psum | solution.py:45
  143.0 0.0 copy-start.1
  143.0 5.2 %copy.24 = f32[4,16,8,17,64]{4,1,3,2,0:T(8,128)} copy(f32[4,16,8,17,64]{4,2,3,1,0:T(8,128)} %get-tuple-element.10) | data formatting | bytes 4456448 | tf_op jit(solution)/shard_map/conv_general_dilated | solution.py:28
  148.2 0.0 copy-done.1
  148.2 0.3 broadcast_subtract_fusion
  148.5 0.8 copy.26
  149.3 2.2 slice.25
  151.6 3.1 %copy.29 = f32[4,16,1,128,64]{3,4,1,0,2:T(8,128)S(1)} copy(f32[4,16,1,128,64]{4,1,3,0,2:T(8,128)} %slice.25) | data formatting | bytes 4194304
  154.6 1.8 fusion.19
  156.4 72.9 %psum.15 = f32[64,64]{1,0:T(8,128)S(1)} all-reduce(f32[64,64]{1,0:T(8,128)S(1)} %fusion.19), channel_id=1, replica_groups=mesh['sx'=8,'sy'=8,'batch'=4] {'sx','sy','batch'}, use_global_device_ids=true, to_apply=%region_2.0 | all-reduce | flops 4096 | bytes 32768 | tf_op jit(solution)/shard_map/psum | solution.py:48
  229.4 0.6 select_reduce_fusion.1
  230.6 0.8 fusion.27
  231.4 0.2 fusion.42
  231.6 0.2 fusion.43
  231.8 0.8 fusion.26
  232.6 0.2 fusion.44
  232.7 0.2 fusion.45
  232.9 0.8 fusion.25
  233.7 0.2 fusion.46
  233.9 0.2 fusion.47
  234.0 0.8 fusion.24
  234.8 0.2 fusion.48
  235.0 0.2 fusion.49
  235.2 4.5 %slice_bitcast_fusion = f32[1,64,4,16,128]{1,3,4,2,0:T(8,128)} fusion(f32[4,16,1,136,64]{4,1,3,0,2:T(8,128)} %bitcast.68), kind=kLoop, calls=%fused_computation.12 | loop fusion | bytes 4194304 | tf_op jit(solution)/shard_map/conv_general_dilated | solution.py:28
  239.7 4.1 %copy.25 = f32[1,64,4,16,128]{4,3,2,1,0:T(8,128)S(1)} copy(f32[1,64,4,16,128]{1,3,4,2,0:T(8,128)} %slice_bitcast_fusion) | data formatting | bytes 4194304 | tf_op jit(solution)/shard_map/conv_general_dilated | solution.py:28
  243.8 0.0 copy-start.3
  243.9 0.0 copy-start.4
  243.9 1.5 reshape.48
  245.4 0.8 fusion.23
  246.2 0.0 copy-done.3
  246.2 0.0 copy-done.4
  246.2 3.9 %fusion.16 = f32[8,8,64,128]{3,1,2,0:T(8,128)S(1)} fusion(f32[64,64]{1,0:T(8,128)S(1)} %fusion.23, f32[64,8192]{1,0:T(8,128)} %reshape.48, f32[64]{0:T(128)S(1)} %copy-done.3, f32[64]{0:T(128)S(1)} %broadcast_multiply_fusion, f32[64]{0:T(128)S(1)} %copy-done.4), kind=kOutput, calls=%fused_computation.20 | convolution fusion | flops 404226048 | bytes 4211456 | tf_op jit(solution)/shard_map/cd,sdn->scn/dot_general | solution.py:57
  250.1 1.7 copy.31
  (4 shorter events, 0.1 us)
Async XLA Ops:
  0.0 45.3 %copy-start = (bf16[64,64,3,3,3]{1,0,4,3,2:T(8,128)(2,1)S(1)}, bf16[64,64,3,3,3]{1,0,4,3,2:T(8,128)(2,1)}, u32[]{:S(2)}) copy-start(bf16[64,64,3,3,3]{1,0,4,3,2:T(8,128)(2,1)} %param.5) | copy-start | bytes 663556
  0.0 10.6 %copy-start.2 = (bf16[1,64,4,16,128]{4,3,2,1,0:T(8,128)(2,1)S(1)}, bf16[1,64,4,16,128]{4,3,2,1,0:T(8,128)(2,1)}, u32[]{:S(2)}) copy-start(bf16[1,64,4,16,128]{4,3,2,1,0:T(8,128)(2,1)} %param.4) | copy-start | bytes 3145732
  1.3 9.3 %collective-permute-start = (bf16[1,64,1,16,128]{4,1,3,2,0:T(8,128)(2,1)S(1)}, bf16[1,64,1,16,128]{4,1,3,2,0:T(8,128)(2,1)S(1)}, u32[]{:S(2)}, u32[]{:S(2)}) collective-permute-start(bf16[1,64,1,16,128]{4,1,3,2,0:T(8,128)(2,1)S(1)} %copy.33), channel_id=1, source_target_pairs={{0,32},{32,64},{64,96},{96,128},{128,160},{160,192},{192,224},{1,3... | collective-permute-start | bytes 786440 | tf_op jit(solution)/shard_map/ppermute | solution.py:17
  5.7 9.1 %collective-permute-start.1 = (bf16[1,64,1,16,128]{4,1,3,2,0:T(8,128)(2,1)S(1)}, bf16[1,64,1,16,128]{4,1,3,2,0:T(8,128)(2,1)S(1)}, u32[]{:S(2)}, u32[]{:S(2)}) collective-permute-start(bf16[1,64,1,16,128]{4,1,3,2,0:T(8,128)(2,1)S(1)} %copy.34), channel_id=1, source_target_pairs={{32,0},{64,32},{96,64},{128,96},{160,128},{192,160},{224,192},{33,... | collective-permute-start | bytes 786440 | tf_op jit(solution)/shard_map/ppermute | solution.py:19
  14.9 6.9 %collective-permute-start.2 = (bf16[1,64,6,1,128]{4,1,3,2,0:T(8,128)(2,1)S(1)}, bf16[1,64,6,1,128]{4,1,3,2,0:T(8,128)(2,1)S(1)}, u32[]{:S(2)}, u32[]{:S(2)}) collective-permute-start(bf16[1,64,6,1,128]{4,1,3,2,0:T(8,128)(2,1)S(1)} %get-tuple-element.5), channel_id=1, source_target_pairs={{0,4},{4,8},{8,12},{12,16},{16,20},{20,24},{24,28},{1,5},{5,9},{9,... | collective-permute-start | bytes 294920 | tf_op jit(solution)/shard_map/ppermute | solution.py:17
  19.7 5.9 %collective-permute-start.3 = (bf16[1,64,6,1,128]{4,1,3,2,0:T(8,128)(2,1)S(1)}, bf16[1,64,6,1,128]{4,1,3,2,0:T(8,128)(2,1)S(1)}, u32[]{:S(2)}, u32[]{:S(2)}) collective-permute-start(bf16[1,64,6,1,128]{4,1,3,2,0:T(8,128)(2,1)S(1)} %get-tuple-element.6), channel_id=1, source_target_pairs={{4,0},{8,4},{12,8},{16,12},{20,16},{24,20},{28,24},{5,1},{9,5},{13... | collective-permute-start | bytes 294920 | tf_op jit(solution)/shard_map/ppermute | solution.py:19
  42.0 3.3 %copy-start.5 = (pred[8,17]{0,1:T(8,128)(4,1)S(1)}, pred[8,17]{0,1:T(8,128)(4,1)}, u32[]{:S(2)}) copy-start(pred[8,17]{0,1:T(8,128)(4,1)} %constant.25) | copy-start | bytes 412
  143.0 5.2 %copy-start.1 = (f32[4,16,8,17,64]{4,2,3,1,0:T(8,128)S(1)}, f32[4,16,8,17,64]{4,2,3,1,0:T(8,128)}, u32[]{:S(2)}) copy-start(f32[4,16,8,17,64]{4,2,3,1,0:T(8,128)} %get-tuple-element.10) | copy-start | bytes 6684676
  243.8 2.3 copy-start.3
  243.9 2.3 copy-start.4
where the time goes:
time: 252 us
  blocking collectives  152 us (60%)
  local copies, waits for them, and re-layouts  44.8 us (18%)
  matrix products  29.4 us (12%)
  starting transfers between devices  12.4 us (5%)
  waiting for transfers between devices  10.8 us (4%)
    psum x1, blocking collectives, on_device(): channel_mean = lax.psum(local_sum, ('sx', 'sy', 'batch')) / total_count  79.4 us
    psum x1, blocking collectives, on_device(): covariance = lax.psum(products, ('sx', 'sy', 'batch')) / total_count  72.9 us
    conv_general_dilated x6, local copies, waits for them, and re-layouts, on_device(): lax.conv_general_dilated(extended, conv_weight, (1, 1, 1), [(0, 0), (0, 0...  25 us
    conv_general_dilated x1, matrix products, on_device(): lax.conv_general_dilated(extended, conv_weight, (1, 1, 1), [(0, 0), (0, 0...  18.2 us
    ppermute x2, starting transfers between devices, extended_2(): lax.ppermute(tail, axis, [(i, (i + 1) % count) for i in range(ends)])  9.15 us
    unnamed x19, local copies, waits for them, and re-layouts  8.63 us
    ppermute x2, waiting for transfers between devices, extended_2(): lax.ppermute(head, axis, [((i + 1) % count, i) for i in range(ends)])  7.32 us
    concatenate x2, local copies, waits for them, and re-layouts, extended_2(): jnp.concatenate([lax.ppermute(tail, axis, [(i, (i + 1) % count) for i in...  5.47 us
  transfers between devices with their start and end apart: 4, of which 3 were waited for; matrix products, arithmetic and copies ran while one was open for 0% of the time, Pallas kernels for 0%

commit v1 on v0

v1 whole, which is shorter than its diff:
```python
import jax
import jax.numpy as jnp
from jax import lax
from jax.experimental import pallas as pl
from jax.experimental.pallas import tpu as pltpu
from jax.sharding import PartitionSpec as P

NS_ITERS = 5
C = 64
BX = 4
BY = 16
NZ = 128
LOCAL = BX * BY * NZ
MESH = pl.DeviceIdType.MESH
F32 = jnp.float32
BF16 = jnp.bfloat16
HIGHEST = lax.Precision.HIGHEST
PAIRS = ((1, 2), (0, 3))


def split(v):
    hi = v.astype(BF16)
    lo = (v - hi.astype(F32)).astype(BF16)
    return hi, lo


def nn(a, b):
    return lax.dot_general(a, b, (((1,), (0,)), ((), ())), preferred_element_type=F32)


def mm(a, b):
    ah, al = split(a)
    bh, bl = split(b)
    return nn(ah, bh) + (nn(ah, bl) + nn(al, bh))


def body(
    sizes,
    vol,
    weight,
    gain,
    shift,
    out,
    vin,
    wide,
    cells,
    win,
    toep,
    held,
    gram,
    sums,
    centre,
    moved_y,
    moved_b,
    moved_x,
    staged,
    vec,
    load_sem,
    wsem,
    vsem,
    xs_send,
    xs_recv,
    ys_send,
    ys_recv,
    cs_send,
    cs_recv,
    ry_send,
    ry_recv,
    rb_send,
    rb_recv,
    rx_send,
    rx_recv,
    out_sem,
):
    n_x, n_y, n_b = sizes
    sx = lax.axis_index("sx")
    sy = lax.axis_index("sy")
    sb = lax.axis_index("batch")

    def at(n, i, k):
        return lax.rem(i + (k + n), n)

    loads = []
    for k, x in enumerate((0, 3, 1, 2)):
        cp = pltpu.make_async_copy(vol.at[0, :, x], vin.at[x], load_sem.at[k])
        cp.start()
        loads.append(cp)
    wcp = pltpu.make_async_copy(weight, win, wsem)
    wcp.start()
    gcp = pltpu.make_async_copy(gain, vec.at[pl.ds(0, 1)], vsem.at[0])
    gcp.start()
    hcp = pltpu.make_async_copy(shift, vec.at[pl.ds(1, 1)], vsem.at[1])
    hcp.start()

    barrier = pltpu.get_barrier_semaphore()
    greeted = 0
    for k in range(1, n_x):
        pl.semaphore_signal(barrier, inc=1, device_id={"sx": at(n_x, sx, k)}, device_id_type=MESH)
        greeted += 1
    for k in range(1, n_y):
        pl.semaphore_signal(barrier, inc=1, device_id={"sy": at(n_y, sy, k)}, device_id_type=MESH)
        greeted += 1
    for k in range(1, n_b):
        pl.semaphore_signal(barrier, inc=1, device_id={"batch": at(n_b, sb, k)}, device_id_type=MESH)
        greeted += 1
    for dx in (-1, 1):
        for dy in (-1, 1):
            pl.semaphore_signal(
                barrier,
                inc=1,
                device_id={"sx": at(n_x, sx, dx), "sy": at(n_y, sy, dy)},
                device_id_type=MESH,
            )
            greeted += 1

    def relay(x):
        wide[...] = vin[x].astype(F32).reshape(C * BY, NZ)
        for y in range(BY):
            cells[x + 1, y + 1] = wide[pl.ds(y, C, stride=BY), :].astype(BF16)

    loads[0].wait()
    relay(0)
    loads[1].wait()
    relay(3)
    pl.semaphore_wait(barrier, greeted)

    sends = []

    def send(src, dst, s_sem, r_sem, dev):
        cp = pltpu.make_async_remote_copy(
            src_ref=src, dst_ref=dst, send_sem=s_sem, recv_sem=r_sem, device_id=dev, device_id_type=MESH
        )
        cp.start()
        sends.append(cp)
        return cp

    xcopies = []
    for q in range(4):
        rows = pl.ds(1 + 4 * q, 4)
        for d, (src_x, dst_x) in enumerate(((1, BX + 1), (BX, 0))):
            xcopies.append(
                send(
                    cells.at[src_x, rows],
                    cells.at[dst_x, rows],
                    xs_send.at[2 * q + d],
                    xs_recv.at[2 * q + d],
                    {"sx": at(n_x, sx, 2 * d - 1)},
                )
            )
    ccopies = []
    for d, (src_x, dst_x) in enumerate(((1, BX + 1), (BX, 0))):
        for f, (src_y, dst_y) in enumerate(((1, BY + 1), (BY, 0))):
            ccopies.append(
                send(
                    cells.at[src_x, src_y],
                    cells.at[dst_x, dst_y],
                    cs_send.at[2 * d + f],
                    cs_recv.at[2 * d + f],
                    {"sx": at(n_x, sx, 2 * d - 1), "sy": at(n_y, sy, 2 * f - 1)},
                )
            )

    loads[2].wait()
    relay(1)
    loads[3].wait()
    relay(2)
    ycopies = []
    for f, (src_y, dst_y) in enumerate(((1, BY + 1), (BY, 0))):
        ycopies.append(
            send(
                cells.at[pl.ds(1, BX), src_y],
                cells.at[pl.ds(1, BX), dst_y],
                ys_send.at[f],
                ys_recv.at[f],
                {"sy": at(n_y, sy, 2 * f - 1)},
            )
        )

    wcp.wait()
    zero = jnp.zeros((C, C), F32)
    for a in range(3):
        for e in range(3):
            w = [win[(a * 3 + b) * 3 + e].astype(F32) for b in range(3)]
            blocks = (
                ((w[0], w[1]), (w[2], zero)),
                ((zero, w[0]), (w[1], w[2])),
            )
            for j in range(2):
                for q in range(2):
                    toep[pl.ds(e * 128 + j * 64, 64), pl.ds(a * 256 + q * 128, 128)] = jnp.concatenate(
                        blocks[j][q], axis=1
                    ).astype(BF16)

    lane = lax.broadcasted_iota(jnp.int32, (C, 128), 1)
    row = lax.broadcasted_iota(jnp.int32, (C, 128), 0)
    eye2 = (lax.rem(lane, C) == row).astype(F32)

    def conv(pair, p):
        pieces = []
        for a in range(3):
            for i in range(4):
                pieces.append(
                    jnp.concatenate([cells[x + a, 2 * p + i] for x in PAIRS[pair]], axis=1)
                )
        d = nn(toep[...], jnp.concatenate(pieces, axis=0))
        parts = []
        for h in range(2):
            for j in range(2):
                t = [
                    d[e * 128 + j * 64 : e * 128 + j * 64 + 64, h * 128 : h * 128 + 128] for e in range(3)
                ]
                before = jnp.where(lane == 0, 0.0, pltpu.roll(t[0], 1, 1))
                after = jnp.where(lane == NZ - 1, 0.0, pltpu.roll(t[2], NZ - 1, 1))
                parts.append(before + t[1] + after)
        return parts

    def keep(pair, p, parts):
        c = centre[...]
        parts = [v - c for v in parts]
        sums[...] += (parts[0] + parts[1]) + (parts[2] + parts[3])
        hi, lo = split(jnp.concatenate(parts, axis=1))
        both = jnp.concatenate([hi, lo], axis=0)
        held[pair * 8 + p] = both
        gram[...] += lax.dot_general(both, both, (((1,), (1,)), ((), ())), preferred_element_type=F32)

    gram[...] = jnp.zeros_like(gram)
    sums[...] = jnp.zeros_like(sums)
    first = conv(0, 1)
    total = (first[0] + first[1]) + (first[2] + first[3])
    mean0 = jnp.sum(total, axis=1, keepdims=True) * (1.0 / 512)
    centre[...] = jnp.broadcast_to(mean0, (C, 128))
    keep(0, 1, first)

    def one(pair, p):
        keep(pair, p, conv(pair, p))

    def several(pair, lo, hi):
        def step(p, carry):
            one(pair, p)
            return carry

        lax.fori_loop(lo, hi, step, 0)

    several(0, 2, 7)

    def clear(cond, x, y, nx, ny):
        @pl.when(cond)
        def _():
            cells[pl.ds(x, nx), pl.ds(y, ny)] = jnp.zeros((nx, ny, C, NZ), BF16)

    x_first, x_last = sx == 0, sx == n_x - 1
    y_first, y_last = sy == 0, sy == n_y - 1
    ycopies[0].wait_recv()
    clear(y_last, 1, BY + 1, BX, 1)
    ycopies[1].wait_recv()
    clear(y_first, 1, 0, BX, 1)
    several(0, 0, 1)
    several(0, 7, 8)

    def arrive(q):
        xcopies[2 * q].wait_recv()
        clear(x_last, BX + 1, 1 + 4 * q, 1, 4)
        xcopies[2 * q + 1].wait_recv()
        clear(x_first, 0, 1 + 4 * q, 1, 4)

    arrive(0)
    arrive(1)
    several(1, 1, 3)
    arrive(2)
    several(1, 3, 5)
    arrive(3)
    several(1, 5, 7)
    for d, (x, x_edge) in enumerate(((BX + 1, x_last), (0, x_first))):
        for f, (y, y_edge) in enumerate(((BY + 1, y_last), (0, y_first))):
            ccopies[2 * d + f].wait_recv()
            clear(jnp.logical_or(x_edge, y_edge), x, y, 1, 1)
    several(1, 0, 1)
    several(1, 7, 8)

    lane32 = lane[:32]

    def pack(v):
        return jnp.where(lane32 < C, v[:32], v[32:])

    def turned(col):
        return jnp.sum(eye2 * col, axis=0, keepdims=True)

    dcol = jnp.sum(sums[...], axis=1, keepdims=True) * (1.0 / LOCAL)
    drow = turned(dcol)
    crow = turned(centre[:, 0:1])
    g = gram[:C] + gram[C:]
    g = g + pltpu.roll(g, C, 1)
    products = pack(g - LOCAL * (dcol * drow))
    mean = crow + drow
    row8 = lax.broadcasted_iota(jnp.int32, (8, 128), 0)

    def merge(products, mean, count, axis, n, me, moved, s_sem, r_sem):
        moved[me, pl.ds(0, 32)] = products
        moved[me, pl.ds(32, 8)] = jnp.where(row8 == me, mean, 0.0)
        copies = [
            send(moved.at[me], moved.at[me], s_sem.at[k - 1], r_sem.at[k - 1], {axis: at(n, me, k)})
            for k in range(1, n)
        ]
        for cp in copies:
            cp.wait_recv()
        total = moved[0]
        for i in range(1, n):
            total = total + moved[i]
        means = total[32:]
        mean = jnp.sum(means, axis=0, keepdims=True) * (1.0 / n)
        off = jnp.where(row8 < n, means - mean, 0.0)
        outer = lax.dot_general(
            off, off, (((0,), (0,)), ((), ())), precision=HIGHEST, preferred_element_type=F32
        )
        return total[:32] + count * pack(outer[:C]), mean

    products, mean = merge(products, mean, float(LOCAL), "sy", n_y, sy, moved_y, ry_send, ry_recv)
    products, mean = merge(products, mean, float(LOCAL * n_y), "batch", n_b, sb, moved_b, rb_send, rb_recv)
    products, mean = merge(products, mean, float(LOCAL * n_y * n_b), "sx", n_x, sx, moved_x, rx_send, rx_recv)

    full = jnp.concatenate([products, pltpu.roll(products, C, 1)], axis=0)[:, :C]
    eye = eye2[:, :C]
    sigma = full * (1.0 / (LOCAL * n_x * n_y * n_b)) + 1e-05 * eye
    trace = jnp.sum(jnp.sum(sigma * eye, axis=1, keepdims=True), axis=0, keepdims=True)
    t = sigma / trace
    f = None
    for turn in range(NS_ITERS):
        step = 1.5 * eye - 0.5 * t
        f = step if f is None else mm(f, step)
        if turn < NS_ITERS - 1:
            t = mm(mm(t, step), step)
    gcp.wait()
    hcp.wait()
    v = vec[...]
    gain_col = jnp.sum(eye * v[0:1], axis=1, keepdims=True)
    shift_col = jnp.sum(eye * v[1:2], axis=1, keepdims=True)
    whiten = f / jnp.sqrt(trace) * gain_col
    bias = shift_col - jnp.sum(whiten * (mean - crow)[:, :C], axis=1, keepdims=True)
    bias = jnp.broadcast_to(bias, (C, 128))
    wh, wl = split(whiten)
    mixer = jnp.concatenate([wh.astype(F32), wh.astype(F32), wl.astype(F32)], axis=1).astype(BF16)

    def mix(pair, p):
        both = held[pair * 8 + p]
        got = nn(mixer, jnp.concatenate([both, both[:C]], axis=0))
        for h in range(2):
            for j in range(2):
                k = 2 * h + j
                staged[pl.ds(PAIRS[pair][h] * BY + 2 * p + j, C, stride=BX * BY), :] = (
                    got[:, k * 128 : k * 128 + 128] + bias
                )

    writes = []
    whole = staged.reshape(C, BX * BY, NZ)
    for pair in range(2):
        for part in range(2):

            def step(p, carry):
                mix(pair, p)
                return carry

            lax.fori_loop(part * 4, part * 4 + 4, step, 0)
            for x in PAIRS[pair]:
                rows = pl.ds(x * BY + part * 8, 8)
                cp = pltpu.make_async_copy(whole.at[:, rows], out.at[:, rows], out_sem.at[len(writes)])
                cp.start()
                writes.append(cp)
    for cp in writes:
        cp.wait()
    for cp in sends:
        cp.wait_send()


def on_device(volume, conv_weight, out_gain, out_shift):
    n_x, n_y, n_b = (lax.axis_size(a) for a in ("sx", "sy", "batch"))
    weight = jnp.transpose(conv_weight, (2, 3, 4, 0, 1)).reshape(27, C, C)
    anywhere = pl.BlockSpec(memory_space=pl.ANY)
    dma = pltpu.SemaphoreType.DMA
    result = pl.pallas_call(
        lambda *refs: body((n_x, n_y, n_b), *refs),
        out_shape=jax.ShapeDtypeStruct((C, BX * BY, NZ), F32),
        in_specs=[anywhere] * 4,
        out_specs=anywhere,
        scratch_shapes=[
            pltpu.VMEM((BX, C, BY, NZ), BF16),
            pltpu.VMEM((C * BY, NZ), F32),
            pltpu.VMEM((BX + 2, BY + 2, C, NZ), BF16),
            pltpu.VMEM((27, C, C), BF16),
            pltpu.VMEM((384, 768), BF16),
            pltpu.VMEM((16, 2 * C, 512), BF16),
            pltpu.VMEM((2 * C, 2 * C), F32),
            pltpu.VMEM((C, 128), F32),
            pltpu.VMEM((C, 128), F32),
            pltpu.VMEM((n_y, 40, 128), F32),
            pltpu.VMEM((n_b, 40, 128), F32),
            pltpu.VMEM((n_x, 40, 128), F32),
            pltpu.VMEM((C * BX * BY, NZ), F32),
            pltpu.VMEM((2, C), F32),
            dma((4,)),
            dma,
            dma((2,)),
            dma((8,)),
            dma((8,)),
            dma((2,)),
            dma((2,)),
            dma((4,)),
            dma((4,)),
            dma((n_y - 1,)),
            dma((n_y - 1,)),
            dma((n_b - 1,)),
            dma((n_b - 1,)),
            dma((n_x - 1,)),
            dma((n_x - 1,)),
            dma((8,)),
        ],
        compiler_params=pltpu.CompilerParams(
            collective_id=0, has_side_effects=True, vmem_limit_bytes=40 * 1024 * 1024
        ),
    )(volume, weight, out_gain.reshape(1, C), out_shift.reshape(1, C))
    return result.reshape(1, C, BX, BY, NZ)


def solution(mesh):
    in_specs = (P("batch", None, "sx", "sy", None), P(), P(), P())
    out_specs = P("batch", None, "sx", "sy", None)
    return jax.shard_map(
        on_device, mesh=mesh, in_specs=in_specs, out_specs=out_specs, check_vma=False
    )
```

time: 252 us -> 46.5 us (0.18)
  blocking collectives: 152 us -> 0 us
  Pallas kernels: 0 us -> 41.4 us
  local copies, waits for them, and re-layouts: 44.8 us -> 4.87 us
  matrix products: 29.4 us -> 0 us
  starting transfers between devices: 12.4 us -> 0 us
  waiting for transfers between devices: 10.8 us -> 0 us
    psum x2 -> x0, blocking collectives: 152 us -> none  [the longest x1 79.4 us: on_device(): channel_mean = lax.psum(local_sum, ('sx', 'sy', 'batch')) / total_count]
    pallas_call x0 -> x1, Pallas kernels: none -> 41.4 us  [on_device(): pl.pallas_call(lambda *refs: body((n_x, n_y, n_b), *refs), out_shape=jax....]
    conv_general_dilated x6 -> x0, local copies, waits for them, and re-layouts: 25 us -> none  [on_device(): lax.conv_general_dilated(extended, conv_weight, (1, 1, 1), [(0, 0), (0, 0...]
    conv_general_dilated x1 -> x0, matrix products: 18.2 us -> none  [on_device(): lax.conv_general_dilated(extended, conv_weight, (1, 1, 1), [(0, 0), (0, 0...]
    ppermute x4 -> x0, starting transfers between devices: 12.4 us -> none  [the longest x2 9.15 us: extended_2(): lax.ppermute(tail, axis, [(i, (i + 1) % count) for i in range(ends)])]
    dot_general x17 -> x0, matrix products: 11.1 us -> none  [the longest x5 3.92 us: on_device(): factor = 1.5 * factor - 0.5 * jnp.dot(cubed, normed, precision=highest)]
    ppermute x4 -> x0, waiting for transfers between devices: 10.8 us -> none  [the longest x2 7.32 us: extended_2(): lax.ppermute(head, axis, [((i + 1) % count, i) for i in range(ends)])]
    concatenate x2 -> x0, local copies, waits for them, and re-layouts: 5.47 us -> none  [extended_2(): jnp.concatenate([lax.ppermute(tail, axis, [(i, (i + 1) % count) for i in...]
  transfers between devices with their start and end apart: 4 -> 0, of which waited for: 3 -> 0; matrix products, arithmetic and copies ran while one was open for 0% -> 0% of each run, Pallas kernels for 0% -> 0%
where the time goes in v1:
time: 46.5 us; the launch traced here: 46.3 us
  Pallas kernels  41.4 us (89%)
  local copies, waits for them, and re-layouts  4.87 us (10%)
    pallas_call x1, Pallas kernels, on_device(): pl.pallas_call(lambda *refs: body((n_x, n_y, n_b), *refs), out_shape=jax....  41.4 us
    unnamed x9, local copies, waits for them, and re-layouts  4.87 us

profile of v1, /device:TPU:1, one launch (start us, length us, event | category | flops | bytes accessed | tf_op | source)
XLA Modules:
  0.0 46.3 jit_solution(18125585788058049992)
XLA Ops:
  0.0 0.0 copy-start
  0.0 1.2 %copy-done = bf16[1,64,4,16,128]{4,3,2,1,0:T(8,128)(2,1)S(1)} copy-done((bf16[1,64,4,16,128]{4,3,2,1,0:T(8,128)(2,1)S(1)}, bf16[1,64,4,16,128]{4,3,2,1,0:T(8,128)(2,1)}, u32[]{:S(2)}) %copy-start) | copy-done | bytes 1048600
  1.2 0.0 copy-start.1
  1.2 1.0 %copy-done.1 = bf16[64,64,3,3,3]{1,0,4,3,2:T(8,128)(2,1)S(1)} copy-done((bf16[64,64,3,3,3]{1,0,4,3,2:T(8,128)(2,1)S(1)}, bf16[64,64,3,3,3]{1,0,4,3,2:T(8,128)(2,1)}, u32[]{:S(2)}) %copy-start.1) | copy-done | bytes 221208
  2.2 0.0 copy-start.2
  2.2 0.7 %copy-done.2 = f32[64]{0:T(128)S(1)} copy-done((f32[64]{0:T(128)S(1)}, f32[64]{0:T(128)}, u32[]{:S(2)}) %copy-start.2) | copy-done | bytes 280
  2.9 0.0 copy-start.3
  2.9 0.7 %copy-done.3 = f32[64]{0:T(128)S(1)} copy-done((f32[64]{0:T(128)S(1)}, f32[64]{0:T(128)}, u32[]{:S(2)}) %copy-start.3) | copy-done | bytes 280
  3.6 41.4 %shard_map.46 = f32[64,64,128]{2,1,0:T(8,128)S(1)} custom-call(bf16[1,64,4,16,128]{4,3,2,1,0:T(8,128)(2,1)S(1)} %copy-done, bf16[27,64,64]{2,1,0:T(8,128)(2,1)S(1)} %bitcast.7, f32[1,64]{1,0:T(1,128)S(1)} %bitcast.8, f32[1,64]{1,0:T(1,128)S(1)} %bitcast.9), custom_call_target="tpu_custom_call" | custom-call | tf_op jit(solution)/shard_map/pallas_call | solution.py:379
  45.0 1.3 %copy.6 = f32[1,64,4,16,128]{4,3,2,1,0:T(8,128)} copy(f32[1,64,4,16,128]{4,3,2,1,0:T(8,128)S(1)} %bitcast.6) | data formatting | bytes 4194304
Async XLA Ops:
  0.0 1.2 %copy-start = (bf16[1,64,4,16,128]{4,3,2,1,0:T(8,128)(2,1)S(1)}, bf16[1,64,4,16,128]{4,3,2,1,0:T(8,128)(2,1)}, u32[]{:S(2)}) copy-start(bf16[1,64,4,16,128]{4,3,2,1,0:T(8,128)(2,1)} %refs_0_.1) | copy-start | bytes 3145732
  1.2 1.0 %copy-start.1 = (bf16[64,64,3,3,3]{1,0,4,3,2:T(8,128)(2,1)S(1)}, bf16[64,64,3,3,3]{1,0,4,3,2:T(8,128)(2,1)}, u32[]{:S(2)}) copy-start(bf16[64,64,3,3,3]{1,0,4,3,2:T(8,128)(2,1)} %param.5) | copy-start | bytes 663556
  2.2 0.7 %copy-start.2 = (f32[64]{0:T(128)S(1)}, f32[64]{0:T(128)}, u32[]{:S(2)}) copy-start(f32[64]{0:T(128)} %param.6) | copy-start | bytes 772
  2.9 0.7 %copy-start.3 = (f32[64]{0:T(128)S(1)}, f32[64]{0:T(128)}, u32[]{:S(2)}) copy-start(f32[64]{0:T(128)} %param.7) | copy-start | bytes 772

commit v2 on v1

--- a/solution.py
+++ b/solution.py
@@ -40,20 +40,20 @@
     weight,
     gain,
     shift,
-    out,
+    held,
+    mixer,
+    offset,
     vin,
     wide,
     cells,
     win,
     toep,
-    held,
     gram,
     sums,
     centre,
-    moved_y,
-    moved_b,
+    moved_c,
+    moved_p,
     moved_x,
-    staged,
     vec,
     load_sem,
     wsem,
@@ -64,13 +64,12 @@
     ys_recv,
     cs_send,
     cs_recv,
-    ry_send,
-    ry_recv,
-    rb_send,
-    rb_recv,
+    rc_send,
+    rc_recv,
+    rp_send,
+    rp_recv,
     rx_send,
     rx_recv,
-    out_sem,
 ):
     n_x, n_y, n_b = sizes
     sx = lax.axis_index("sx")
@@ -92,26 +91,25 @@
     hcp = pltpu.make_async_copy(shift, vec.at[pl.ds(1, 1)], vsem.at[1])
     hcp.start()
 
+    n_chip = n_y // 2
+    core = lax.rem(sy, 2)
+    chip = sy // 2
+    sibling = {"sy": sy + (1 - 2 * core)}
+    others_x = [{"sx": at(n_x, sx, k)} for k in sorted(range(1, n_x), key=lambda k: -min(k, n_x - k))]
+    plane = sorted(
+        ((j, k) for j in range(n_chip) for k in range(n_b) if j or k),
+        key=lambda o: -min(o[0], n_chip - o[0]) - min(o[1], n_b - o[1]),
+    )
+    others_p = [{"sy": 2 * at(n_chip, chip, j) + core, "batch": at(n_b, sb, k)} for j, k in plane]
+    diagonal = [
+        {"sx": at(n_x, sx, dx), "sy": at(n_y, sy, dy)} for dx in (-1, 1) for dy in (-1, 1)
+    ]
+    beside = {"sy": at(n_y, sy, 2 * core - 1)}
+
     barrier = pltpu.get_barrier_semaphore()
-    greeted = 0
-    for k in range(1, n_x):
-        pl.semaphore_signal(barrier, inc=1, device_id={"sx": at(n_x, sx, k)}, device_id_type=MESH)
-        greeted += 1
-    for k in range(1, n_y):
-        pl.semaphore_signal(barrier, inc=1, device_id={"sy": at(n_y, sy, k)}, device_id_type=MESH)
-        greeted += 1
-    for k in range(1, n_b):
-        pl.semaphore_signal(barrier, inc=1, device_id={"batch": at(n_b, sb, k)}, device_id_type=MESH)
-        greeted += 1
-    for dx in (-1, 1):
-        for dy in (-1, 1):
-            pl.semaphore_signal(
-                barrier,
-                inc=1,
-                device_id={"sx": at(n_x, sx, dx), "sy": at(n_y, sy, dy)},
-                device_id_type=MESH,
-            )
-            greeted += 1
+    greeted = [sibling, beside] + others_x + diagonal + others_p
+    for device in greeted:
+        pl.semaphore_signal(barrier, inc=1, device_id=device, device_id_type=MESH)
 
     def relay(x):
         wide[...] = vin[x].astype(F32).reshape(C * BY, NZ)
@@ -122,7 +120,7 @@
     relay(0)
     loads[1].wait()
     relay(3)
-    pl.semaphore_wait(barrier, greeted)
+    pl.semaphore_wait(barrier, len(greeted))
 
     sends = []
 
@@ -134,19 +132,11 @@
         sends.append(cp)
         return cp
 
-    xcopies = []
-    for q in range(4):
-        rows = pl.ds(1 + 4 * q, 4)
-        for d, (src_x, dst_x) in enumerate(((1, BX + 1), (BX, 0))):
-            xcopies.append(
-                send(
-                    cells.at[src_x, rows],
-                    cells.at[dst_x, rows],
-                    xs_send.at[2 * q + d],
-                    xs_recv.at[2 * q + d],
-                    {"sx": at(n_x, sx, 2 * d - 1)},
-                )
-            )
+    def piece(q):
+        start = 1 if q == 0 else 2 * q + 2
+        stop = min(2 * q + 4, BY + 1)
+        return pl.ds(start, stop - start)
+
     ccopies = []
     for d, (src_x, dst_x) in enumerate(((1, BX + 1), (BX, 0))):
         for f, (src_y, dst_y) in enumerate(((1, BY + 1), (BY, 0))):
@@ -157,6 +147,20 @@
                     cs_send.at[2 * d + f],
                     cs_recv.at[2 * d + f],
                     {"sx": at(n_x, sx, 2 * d - 1), "sy": at(n_y, sy, 2 * f - 1)},
+                )
+            )
+
+    xcopies = []
+    for q in range(8):
+        rows = piece(q)
+        for d, (src_x, dst_x) in enumerate(((1, BX + 1), (BX, 0))):
+            xcopies.append(
+                send(
+                    cells.at[src_x, rows],
+                    cells.at[dst_x, rows],
+                    xs_send.at[2 * q + d],
+                    xs_recv.at[2 * q + d],
+                    {"sx": at(n_x, sx, 2 * d - 1)},
                 )
             )
 
@@ -235,11 +239,8 @@
         keep(pair, p, conv(pair, p))
 
     def several(pair, lo, hi):
-        def step(p, carry):
+        for p in range(lo, hi):
             one(pair, p)
-            return carry
-
-        lax.fori_loop(lo, hi, step, 0)
 
     several(0, 2, 7)
 
@@ -257,68 +258,86 @@
     several(0, 0, 1)
     several(0, 7, 8)
 
-    def arrive(q):
-        xcopies[2 * q].wait_recv()
-        clear(x_last, BX + 1, 1 + 4 * q, 1, 4)
-        xcopies[2 * q + 1].wait_recv()
-        clear(x_first, 0, 1 + 4 * q, 1, 4)
-
-    arrive(0)
-    arrive(1)
-    several(1, 1, 3)
-    arrive(2)
-    several(1, 3, 5)
-    arrive(3)
-    several(1, 5, 7)
-    for d, (x, x_edge) in enumerate(((BX + 1, x_last), (0, x_first))):
-        for f, (y, y_edge) in enumerate(((BY + 1, y_last), (0, y_first))):
+    def corner(f, y, y_edge):
+        for d, (x, x_edge) in enumerate(((BX + 1, x_last), (0, x_first))):
             ccopies[2 * d + f].wait_recv()
             clear(jnp.logical_or(x_edge, y_edge), x, y, 1, 1)
-    several(1, 0, 1)
-    several(1, 7, 8)
-
-    lane32 = lane[:32]
-
-    def pack(v):
-        return jnp.where(lane32 < C, v[:32], v[32:])
+
+    corner(1, 0, y_first)
+    corner(0, BY + 1, y_last)
+    for q in range(8):
+        rows = piece(q)
+        xcopies[2 * q].wait_recv()
+        clear(x_last, BX + 1, rows.start, 1, rows.size)
+        xcopies[2 * q + 1].wait_recv()
+        clear(x_first, 0, rows.start, 1, rows.size)
+        one(1, q)
 
     def turned(col):
         return jnp.sum(eye2 * col, axis=0, keepdims=True)
+
+    H = C // 2
+    lane32, row32 = lane[:H], row[:H]
+    low = lax.rem(lane32, C)
+
+    def pack(v):
+        top = v[:H]
+        last = pltpu.roll(v[H:], 128 - H, 1)
+        mixed = jnp.where(jnp.logical_and(low < H, row32 > low), last, top)
+        diag = jnp.sum(jnp.where(low == row32, last, 0.0), axis=0, keepdims=True)
+        return jnp.where(lane32[:16] < C, mixed[:16], mixed[16:]), diag
 
     dcol = jnp.sum(sums[...], axis=1, keepdims=True) * (1.0 / LOCAL)
     drow = turned(dcol)
     crow = turned(centre[:, 0:1])
     g = gram[:C] + gram[C:]
     g = g + pltpu.roll(g, C, 1)
-    products = pack(g - LOCAL * (dcol * drow))
+    products, diag = pack(g - LOCAL * (dcol * drow))
     mean = crow + drow
-    row8 = lax.broadcasted_iota(jnp.int32, (8, 128), 0)
-
-    def merge(products, mean, count, axis, n, me, moved, s_sem, r_sem):
-        moved[me, pl.ds(0, 32)] = products
-        moved[me, pl.ds(32, 8)] = jnp.where(row8 == me, mean, 0.0)
+    lane1 = lane[:1]
+
+    def merge(products, diag, mean, count, n, me, others, moved, s_sem, r_sem):
+        high = moved.shape[1] - 16
+        rows = row[:high]
+        line = jnp.where(lane1 < C, mean, jnp.where(lane1 < C + H, diag, 0.0))
+        moved[me, pl.ds(0, 16)] = products
+        moved[me, pl.ds(16, high)] = jnp.where(rows == me, line, 0.0)
         copies = [
-            send(moved.at[me], moved.at[me], s_sem.at[k - 1], r_sem.at[k - 1], {axis: at(n, me, k)})
-            for k in range(1, n)
+            send(moved.at[me], moved.at[me], s_sem.at[k], r_sem.at[k], device)
+            for k, device in enumerate(others)
         ]
         for cp in copies:
             cp.wait_recv()
         total = moved[0]
         for i in range(1, n):
             total = total + moved[i]
-        means = total[32:]
-        mean = jnp.sum(means, axis=0, keepdims=True) * (1.0 / n)
-        off = jnp.where(row8 < n, means - mean, 0.0)
+        means = total[16:]
+        line = jnp.sum(means, axis=0, keepdims=True)
+        mean = jnp.where(lane1 < C, line * (1.0 / n), 0.0)
+        off = jnp.where(jnp.logical_and(rows < n, lane[:high] < C), means - mean, 0.0)
+        off = off + pltpu.roll(off, C, 1)
         outer = lax.dot_general(
             off, off, (((0,), (0,)), ((), ())), precision=HIGHEST, preferred_element_type=F32
         )
-        return total[:32] + count * pack(outer[:C]), mean
-
-    products, mean = merge(products, mean, float(LOCAL), "sy", n_y, sy, moved_y, ry_send, ry_recv)
-    products, mean = merge(products, mean, float(LOCAL * n_y), "batch", n_b, sb, moved_b, rb_send, rb_recv)
-    products, mean = merge(products, mean, float(LOCAL * n_y * n_b), "sx", n_x, sx, moved_x, rx_send, rx_recv)
-
-    full = jnp.concatenate([products, pltpu.roll(products, C, 1)], axis=0)[:, :C]
+        more, more_diag = pack(outer[:C])
+        return total[:16] + count * more, line + count * more_diag, mean + pltpu.roll(mean, C, 1)
+
+    count = float(LOCAL)
+    state = merge(products, diag, mean, count, 2, core, [sibling], moved_c, rc_send, rc_recv)
+    count *= 2
+    state = merge(
+        *state, count, n_chip * n_b, chip * n_b + sb, others_p, moved_p, rp_send, rp_recv
+    )
+    count *= n_chip * n_b
+    products, diag, mean = merge(*state, count, n_x, sx, others_x, moved_x, rx_send, rx_recv)
+
+    half = jnp.concatenate([products, pltpu.roll(products, C, 1)], axis=0)
+    across = jnp.concatenate([half, jnp.zeros((128 - H, 128), F32)], axis=0).T
+    upper = jnp.where(jnp.logical_and(lane32 < H, row32 > lane32), across[:H], half)
+    last = pltpu.roll(jnp.where(row32 > lane32, half, across[:H]), H, 1)
+    last = jnp.where(lane32 == row32 + H, pltpu.roll(diag, 128 - H, 1), last)
+    lower = jnp.where(lane32 < H, across[H:C], last)
+    full = jnp.concatenate([upper, lower], axis=0)[:, :C]
     eye = eye2[:, :C]
     sigma = full * (1.0 / (LOCAL * n_x * n_y * n_b)) + 1e-05 * eye
     trace = jnp.sum(jnp.sum(sigma * eye, axis=1, keepdims=True), axis=0, keepdims=True)
@@ -336,87 +355,95 @@
     shift_col = jnp.sum(eye * v[1:2], axis=1, keepdims=True)
     whiten = f / jnp.sqrt(trace) * gain_col
     bias = shift_col - jnp.sum(whiten * (mean - crow)[:, :C], axis=1, keepdims=True)
-    bias = jnp.broadcast_to(bias, (C, 128))
+    offset[...] = jnp.broadcast_to(bias, (C, 128))
     wh, wl = split(whiten)
-    mixer = jnp.concatenate([wh.astype(F32), wh.astype(F32), wl.astype(F32)], axis=1).astype(BF16)
-
-    def mix(pair, p):
-        both = held[pair * 8 + p]
-        got = nn(mixer, jnp.concatenate([both, both[:C]], axis=0))
-        for h in range(2):
-            for j in range(2):
-                k = 2 * h + j
-                staged[pl.ds(PAIRS[pair][h] * BY + 2 * p + j, C, stride=BX * BY), :] = (
-                    got[:, k * 128 : k * 128 + 128] + bias
-                )
-
+    mixer[...] = jnp.concatenate([wh.astype(F32), wh.astype(F32), wl.astype(F32)], axis=1).astype(BF16)
+    for cp in sends:
+        cp.wait_send()
+
+
+def mix_body(held, mixer, offset, out, staged, sem):
     writes = []
     whole = staged.reshape(C, BX * BY, NZ)
+    bias = offset[...]
     for pair in range(2):
         for part in range(2):
-
-            def step(p, carry):
-                mix(pair, p)
-                return carry
-
-            lax.fori_loop(part * 4, part * 4 + 4, step, 0)
+            for p in range(part * 4, part * 4 + 4):
+                both = held[pair * 8 + p]
+                got = nn(mixer[...], jnp.concatenate([both, both[:C]], axis=0))
+                for h in range(2):
+                    for j in range(2):
+                        k = 2 * h + j
+                        staged[pl.ds(PAIRS[pair][h] * BY + 2 * p + j, C, stride=BX * BY), :] = (
+                            got[:, k * 128 : k * 128 + 128] + bias
+                        )
             for x in PAIRS[pair]:
                 rows = pl.ds(x * BY + part * 8, 8)
-                cp = pltpu.make_async_copy(whole.at[:, rows], out.at[:, rows], out_sem.at[len(writes)])
+                cp = pltpu.make_async_copy(whole.at[:, rows], out.at[:, rows], sem.at[len(writes)])
                 cp.start()
                 writes.append(cp)
     for cp in writes:
         cp.wait()
-    for cp in sends:
-        cp.wait_send()
 
 
 def on_device(volume, conv_weight, out_gain, out_shift):
     n_x, n_y, n_b = (lax.axis_size(a) for a in ("sx", "sy", "batch"))
     weight = jnp.transpose(conv_weight, (2, 3, 4, 0, 1)).reshape(27, C, C)
     anywhere = pl.BlockSpec(memory_space=pl.ANY)
+    inside = pl.BlockSpec(memory_space=pltpu.VMEM)
     dma = pltpu.SemaphoreType.DMA
-    result = pl.pallas_call(
+    n_p = n_y // 2 * n_b
+    operands = (volume, weight, out_gain.reshape(1, C), out_shift.reshape(1, C))
+    held, mixer, offset = pl.pallas_call(
         lambda *refs: body((n_x, n_y, n_b), *refs),
-        out_shape=jax.ShapeDtypeStruct((C, BX * BY, NZ), F32),
+        out_shape=[
+            jax.ShapeDtypeStruct((16, 2 * C, 512), BF16),
+            jax.ShapeDtypeStruct((C, 3 * C), BF16),
+            jax.ShapeDtypeStruct((C, 128), F32),
+        ],
         in_specs=[anywhere] * 4,
-        out_specs=anywhere,
+        out_specs=[inside] * 3,
         scratch_shapes=[
             pltpu.VMEM((BX, C, BY, NZ), BF16),
             pltpu.VMEM((C * BY, NZ), F32),
             pltpu.VMEM((BX + 2, BY + 2, C, NZ), BF16),
             pltpu.VMEM((27, C, C), BF16),
             pltpu.VMEM((384, 768), BF16),
-            pltpu.VMEM((16, 2 * C, 512), BF16),
             pltpu.VMEM((2 * C, 2 * C), F32),
             pltpu.VMEM((C, 128), F32),
             pltpu.VMEM((C, 128), F32),
-            pltpu.VMEM((n_y, 40, 128), F32),
-            pltpu.VMEM((n_b, 40, 128), F32),
-            pltpu.VMEM((n_x, 40, 128), F32),
-            pltpu.VMEM((C * BX * BY, NZ), F32),
+            pltpu.VMEM((2, 24, 128), F32),
+            pltpu.VMEM((n_p, 32, 128), F32),
+            pltpu.VMEM((n_x, 24, 128), F32),
             pltpu.VMEM((2, C), F32),
             dma((4,)),
             dma,
             dma((2,)),
-            dma((8,)),
-            dma((8,)),
+            dma((16,)),
+            dma((16,)),
             dma((2,)),
             dma((2,)),
             dma((4,)),
             dma((4,)),
-            dma((n_y - 1,)),
-            dma((n_y - 1,)),
-            dma((n_b - 1,)),
-            dma((n_b - 1,)),
+            dma((1,)),
+            dma((1,)),
+            dma((n_p - 1,)),
+            dma((n_p - 1,)),
             dma((n_x - 1,)),
             dma((n_x - 1,)),
-            dma((8,)),
         ],
         compiler_params=pltpu.CompilerParams(
             collective_id=0, has_side_effects=True, vmem_limit_bytes=40 * 1024 * 1024
         ),
-    )(volume, weight, out_gain.reshape(1, C), out_shift.reshape(1, C))
+    )(*(pltpu.with_memory_space_constraint(v, pltpu.HBM) for v in operands))
+    result = pl.pallas_call(
+        mix_body,
+        out_shape=jax.ShapeDtypeStruct((C, BX * BY, NZ), F32),
+        in_specs=[inside] * 3,
+        out_specs=anywhere,
+        scratch_shapes=[pltpu.VMEM((C * BX * BY, NZ), F32), dma((8,))],
+        compiler_params=pltpu.CompilerParams(vmem_limit_bytes=40 * 1024 * 1024),
+    )(held, mixer, offset)
     return result.reshape(1, C, BX, BY, NZ)
 
 

time: 46.5 us -> 38 us (0.82)
  local copies, waits for them, and re-layouts: 4.87 us -> 0 us
  Pallas kernels: 41.4 us -> 37.9 us
    unnamed x9 -> x0, local copies, waits for them, and re-layouts: 4.87 us -> none
    pallas_call x1 -> x2, Pallas kernels: 41.4 us -> 37.9 us  [the longest x1 35.3 us: on_device(): pl.pallas_call(lambda *refs: body((n_x, n_y, n_b), *refs), out_shape=[jax...]
where the time goes in v2:
time: 38 us; the launch traced here: 37.9 us
  Pallas kernels  37.9 us (100%)
    pallas_call x1, Pallas kernels, on_device(): pl.pallas_call(lambda *refs: body((n_x, n_y, n_b), *refs), out_shape=[jax...  35.3 us
    pallas_call x1, Pallas kernels, on_device(): pl.pallas_call(mix_body, out_shape=jax.ShapeDtypeStruct((C, BX * BY, NZ),...  2.57 us

profile of v2, /device:TPU:1, one launch (start us, length us, event | category | flops | bytes accessed | tf_op | source)
XLA Modules:
  0.0 37.9 jit_solution(6704063442421412589)
XLA Ops:
  0.0 35.3 %shard_map.46 = (bf16[16,128,512]{2,1,0:T(8,128)(2,1)S(1)}, bf16[64,192]{1,0:T(8,128)(2,1)S(1)}, f32[64,128]{1,0:T(8,128)S(1)}) custom-call(bf16[1,64,4,16,128]{4,3,2,1,0:T(8,128)(2,1)} %refs_0_.1, bf16[27,64,64]{2,1,0:T(8,128)(2,1)} %bitcast.6, f32[1,64]{1,0:T(1,128)} %bitcast.7, f32[1,64]{1,0:T(1,128)} %bitcast.8), custom_call_target="tpu_custom_call" | custom-call | tf_op jit(solution)/shard_map/pallas_call | solution.py:397
  35.3 2.6 %shard_map.47 = f32[64,64,128]{2,1,0:T(8,128)} custom-call(bf16[16,128,512]{2,1,0:T(8,128)(2,1)S(1)} %get-tuple-element.8.held, bf16[64,192]{1,0:T(8,128)(2,1)S(1)} %get-tuple-element.9.mixer, f32[64,128]{1,0:T(8,128)S(1)} %get-tuple-element.10.offset), custom_call_target="tpu_custom_call" | custom-call | tf_op jit(solution)/shard_map/pallas_call | solution.py:439

commit v3 on v2

--- a/solution.py
+++ b/solution.py
@@ -15,6 +15,7 @@
 F32 = jnp.float32
 BF16 = jnp.bfloat16
 HIGHEST = lax.Precision.HIGHEST
+LAST = (1, 2, 3, 4, 5, 6, 7, 8)
 PAIRS = ((1, 2), (0, 3))
 
 
@@ -107,7 +108,7 @@
     beside = {"sy": at(n_y, sy, 2 * core - 1)}
 
     barrier = pltpu.get_barrier_semaphore()
-    greeted = [sibling, beside] + others_x + diagonal + others_p
+    greeted = others_x[::-1] + diagonal + [beside, sibling] + others_p
     for device in greeted:
         pl.semaphore_signal(barrier, inc=1, device_id=device, device_id_type=MESH)
 
@@ -133,8 +134,8 @@
         return cp
 
     def piece(q):
-        start = 1 if q == 0 else 2 * q + 2
-        stop = min(2 * q + 4, BY + 1)
+        start = 1 if q == 0 else 2 * LAST[q - 1] + 2
+        stop = min(2 * LAST[q] + 2, BY + 1)
         return pl.ds(start, stop - start)
 
     ccopies = []
@@ -151,7 +152,7 @@
             )
 
     xcopies = []
-    for q in range(8):
+    for q in range(len(LAST)):
         rows = piece(q)
         for d, (src_x, dst_x) in enumerate(((1, BX + 1), (BX, 0))):
             xcopies.append(
@@ -265,13 +266,13 @@
 
     corner(1, 0, y_first)
     corner(0, BY + 1, y_last)
-    for q in range(8):
+    for q in range(len(LAST)):
         rows = piece(q)
         xcopies[2 * q].wait_recv()
         clear(x_last, BX + 1, rows.start, 1, rows.size)
         xcopies[2 * q + 1].wait_recv()
         clear(x_first, 0, rows.start, 1, rows.size)
-        one(1, q)
+        several(1, LAST[q - 1] if q else 0, LAST[q])
 
     def turned(col):
         return jnp.sum(eye2 * col, axis=0, keepdims=True)
@@ -363,27 +364,18 @@
 
 
 def mix_body(held, mixer, offset, out, staged, sem):
-    writes = []
-    whole = staged.reshape(C, BX * BY, NZ)
     bias = offset[...]
     for pair in range(2):
-        for part in range(2):
-            for p in range(part * 4, part * 4 + 4):
-                both = held[pair * 8 + p]
-                got = nn(mixer[...], jnp.concatenate([both, both[:C]], axis=0))
-                for h in range(2):
-                    for j in range(2):
-                        k = 2 * h + j
-                        staged[pl.ds(PAIRS[pair][h] * BY + 2 * p + j, C, stride=BX * BY), :] = (
-                            got[:, k * 128 : k * 128 + 128] + bias
-                        )
-            for x in PAIRS[pair]:
-                rows = pl.ds(x * BY + part * 8, 8)
-                cp = pltpu.make_async_copy(whole.at[:, rows], out.at[:, rows], sem.at[len(writes)])
-                cp.start()
-                writes.append(cp)
-    for cp in writes:
-        cp.wait()
+        for p in range(8):
+            both = held[pair * 8 + p]
+            got = nn(mixer[...], jnp.concatenate([both, both[:C]], axis=0))
+            for h in range(2):
+                for j in range(2):
+                    k = 2 * h + j
+                    place = PAIRS[pair][h] * BY + 2 * p + j
+                    staged[place] = got[:, k * 128 : k * 128 + 128] + bias
+                    pltpu.make_async_copy(staged.at[place], out.at[:, place], sem).start()
+    pltpu.make_async_copy(staged, out, sem).wait()
 
 
 def on_device(volume, conv_weight, out_gain, out_shift):
@@ -419,8 +411,8 @@
             dma((4,)),
             dma,
             dma((2,)),
-            dma((16,)),
-            dma((16,)),
+            dma((2 * len(LAST),)),
+            dma((2 * len(LAST),)),
             dma((2,)),
             dma((2,)),
             dma((4,)),
@@ -441,7 +433,7 @@
         out_shape=jax.ShapeDtypeStruct((C, BX * BY, NZ), F32),
         in_specs=[inside] * 3,
         out_specs=anywhere,
-        scratch_shapes=[pltpu.VMEM((C * BX * BY, NZ), F32), dma((8,))],
+        scratch_shapes=[pltpu.VMEM((BX * BY, C, NZ), F32), dma],
         compiler_params=pltpu.CompilerParams(vmem_limit_bytes=40 * 1024 * 1024),
     )(held, mixer, offset)
     return result.reshape(1, C, BX, BY, NZ)

time: 38 us -> 36.9 us (0.971)
  Pallas kernels: 37.9 us -> 36.8 us
    pallas_call x1, Pallas kernels: 2.57 us -> 1.49 us  [on_device(): pl.pallas_call(mix_body, out_shape=jax.ShapeDtypeStruct((C, BX * BY, NZ),...]
where the time goes in v3:
time: 36.9 us
  Pallas kernels  36.8 us (100%)
    pallas_call x1, Pallas kernels, on_device(): pl.pallas_call(lambda *refs: body((n_x, n_y, n_b), *refs), out_shape=[jax...  35.4 us
    pallas_call x1, Pallas kernels, on_device(): pl.pallas_call(mix_body, out_shape=jax.ShapeDtypeStruct((C, BX * BY, NZ),...  1.49 us

profile of v3, /device:TPU:1, one launch (start us, length us, event | category | flops | bytes accessed | tf_op | source)
XLA Modules:
  0.0 36.9 jit_solution(5446744930421548344)
XLA Ops:
  0.0 35.4 %shard_map.46 = (bf16[16,128,512]{2,1,0:T(8,128)(2,1)S(1)}, bf16[64,192]{1,0:T(8,128)(2,1)S(1)}, f32[64,128]{1,0:T(8,128)S(1)}) custom-call(bf16[1,64,4,16,128]{4,3,2,1,0:T(8,128)(2,1)} %refs_0_.1, bf16[27,64,64]{2,1,0:T(8,128)(2,1)} %bitcast.6, f32[1,64]{1,0:T(1,128)} %bitcast.7, f32[1,64]{1,0:T(1,128)} %bitcast.8), custom_call_target="tpu_custom_call" | custom-call | tf_op jit(solution)/shard_map/pallas_call | solution.py:389
  35.4 1.5 %shard_map.47 = f32[64,64,128]{2,1,0:T(8,128)} custom-call(bf16[16,128,512]{2,1,0:T(8,128)(2,1)S(1)} %get-tuple-element.8.held, bf16[64,192]{1,0:T(8,128)(2,1)S(1)} %get-tuple-element.9.mixer, f32[64,128]{1,0:T(8,128)S(1)} %get-tuple-element.10.offset), custom_call_target="tpu_custom_call" | custom-call | tf_op jit(solution)/shard_map/pallas_call | solution.py:431

commit v4 on v3

--- a/solution.py
+++ b/solution.py
@@ -14,7 +14,6 @@
 MESH = pl.DeviceIdType.MESH
 F32 = jnp.float32
 BF16 = jnp.bfloat16
-HIGHEST = lax.Precision.HIGHEST
 LAST = (1, 2, 3, 4, 5, 6, 7, 8)
 PAIRS = ((1, 2), (0, 3))
 
@@ -71,6 +70,7 @@
     rp_recv,
     rx_send,
     rx_recv,
+    known,
 ):
     n_x, n_y, n_b = sizes
     sx = lax.axis_index("sx")
@@ -108,9 +108,22 @@
     beside = {"sy": at(n_y, sy, 2 * core - 1)}
 
     barrier = pltpu.get_barrier_semaphore()
-    greeted = others_x[::-1] + diagonal + [beside, sibling] + others_p
+    near_x = [{"sx": at(n_x, sx, k)} for k in (-1, 1)]
+    near_y = [{"sy": at(n_y, sy, k)} for k in (-2, 2)]
+    near_b = [{"batch": at(n_b, sb, k)} for k in (-1, 1)]
+    greeted = near_x + diagonal + [beside, sibling] + near_y + near_b
     for device in greeted:
         pl.semaphore_signal(barrier, inc=1, device_id=device, device_id_type=MESH)
+
+    def tell(k):
+        for device in near_x:
+            pl.semaphore_signal(known.at[k, 0], inc=1, device_id=device, device_id_type=MESH)
+        for device in near_b if k else near_y:
+            pl.semaphore_signal(known.at[k, 1], inc=1, device_id=device, device_id_type=MESH)
+
+    def hear(k):
+        pl.semaphore_wait(known.at[k, 0], 2)
+        pl.semaphore_wait(known.at[k, 1], 2)
 
     def relay(x):
         wide[...] = vin[x].astype(F32).reshape(C * BY, NZ)
@@ -181,6 +194,7 @@
             )
         )
 
+    tell(0)
     wcp.wait()
     zero = jnp.zeros((C, C), F32)
     for a in range(3):
@@ -243,7 +257,13 @@
         for p in range(lo, hi):
             one(pair, p)
 
-    several(0, 2, 7)
+    several(0, 2, 4)
+    hear(0)
+    tell(1)
+    several(0, 4, 6)
+    hear(1)
+    tell(2)
+    several(0, 6, 7)
 
     def clear(cond, x, y, nx, ny):
         @pl.when(cond)
@@ -264,6 +284,7 @@
             ccopies[2 * d + f].wait_recv()
             clear(jnp.logical_or(x_edge, y_edge), x, y, 1, 1)
 
+    hear(2)
     corner(1, 0, y_first)
     corner(0, BY + 1, y_last)
     for q in range(len(LAST)):
@@ -317,8 +338,13 @@
         mean = jnp.where(lane1 < C, line * (1.0 / n), 0.0)
         off = jnp.where(jnp.logical_and(rows < n, lane[:high] < C), means - mean, 0.0)
         off = off + pltpu.roll(off, C, 1)
+        oh, ol = (v.astype(F32) for v in split(off))
+        rest = [jnp.zeros((8, 128), F32)] * (high == 8)
         outer = lax.dot_general(
-            off, off, (((0,), (0,)), ((), ())), precision=HIGHEST, preferred_element_type=F32
+            jnp.concatenate([oh, oh, ol] + rest, axis=0).astype(BF16),
+            jnp.concatenate([oh, ol, oh] + rest, axis=0).astype(BF16),
+            (((0,), (0,)), ((), ())),
+            preferred_element_type=F32,
         )
         more, more_diag = pack(outer[:C])
         return total[:16] + count * more, line + count * more_diag, mean + pltpu.roll(mean, C, 1)
@@ -423,6 +449,7 @@
             dma((n_p - 1,)),
             dma((n_x - 1,)),
             dma((n_x - 1,)),
+            pltpu.SemaphoreType.REGULAR((3, 2)),
         ],
         compiler_params=pltpu.CompilerParams(
             collective_id=0, has_side_effects=True, vmem_limit_bytes=40 * 1024 * 1024

time: 36.9 us -> 36.3 us (0.984)
  Pallas kernels: 36.8 us -> 36.2 us
    pallas_call x1, Pallas kernels: 35.4 us -> 34.8 us  [on_device(): pl.pallas_call(lambda *refs: body((n_x, n_y, n_b), *refs), out_shape=[jax...]
where the time goes in v4:
time: 36.3 us
  Pallas kernels  36.2 us (100%)
    pallas_call x1, Pallas kernels, on_device(): pl.pallas_call(lambda *refs: body((n_x, n_y, n_b), *refs), out_shape=[jax...  34.8 us
    pallas_call x1, Pallas kernels, on_device(): pl.pallas_call(mix_body, out_shape=jax.ShapeDtypeStruct((C, BX * BY, NZ),...  1.49 us

profile of v4, /device:TPU:1, one launch (start us, length us, event | category | flops | bytes accessed | tf_op | source)
XLA Modules:
  0.0 36.3 jit_solution(10421524068126473375)
XLA Ops:
  0.0 34.8 %shard_map.46 = (bf16[16,128,512]{2,1,0:T(8,128)(2,1)S(1)}, bf16[64,192]{1,0:T(8,128)(2,1)S(1)}, f32[64,128]{1,0:T(8,128)S(1)}) custom-call(bf16[1,64,4,16,128]{4,3,2,1,0:T(8,128)(2,1)} %refs_0_.1, bf16[27,64,64]{2,1,0:T(8,128)(2,1)} %bitcast.6, f32[1,64]{1,0:T(1,128)} %bitcast.7, f32[1,64]{1,0:T(1,128)} %bitcast.8), custom_call_target="tpu_custom_call" | custom-call | tf_op jit(solution)/shard_map/pallas_call | solution.py:415
  34.8 1.5 %shard_map.47 = f32[64,64,128]{2,1,0:T(8,128)} custom-call(bf16[16,128,512]{2,1,0:T(8,128)(2,1)S(1)} %get-tuple-element.8.held, bf16[64,192]{1,0:T(8,128)(2,1)S(1)} %get-tuple-element.9.mixer, f32[64,128]{1,0:T(8,128)S(1)} %get-tuple-element.10.offset), custom_call_target="tpu_custom_call" | custom-call | tf_op jit(solution)/shard_map/pallas_call | solution.py:458

commit v5 on v4

--- a/solution.py
+++ b/solution.py
@@ -14,7 +14,8 @@
 MESH = pl.DeviceIdType.MESH
 F32 = jnp.float32
 BF16 = jnp.bfloat16
-LAST = (1, 2, 3, 4, 5, 6, 7, 8)
+PIECES = ((1, 1), (16, 1), (2, 4), (6, 2), (8, 2), (10, 2), (12, 2), (14, 2))
+READY = ((), (), (1,), (2,), (3, 0), (4,), (5,), (6, 7))
 PAIRS = ((1, 2), (0, 3))
 
 
@@ -31,7 +32,8 @@
 def mm(a, b):
     ah, al = split(a)
     bh, bl = split(b)
-    return nn(ah, bh) + (nn(ah, bl) + nn(al, bh))
+    both = nn(jnp.concatenate([ah, al], axis=0), bh)
+    return both[:C] + (both[C:] + nn(ah, bl))
 
 
 def body(
@@ -102,16 +104,13 @@
         key=lambda o: -min(o[0], n_chip - o[0]) - min(o[1], n_b - o[1]),
     )
     others_p = [{"sy": 2 * at(n_chip, chip, j) + core, "batch": at(n_b, sb, k)} for j, k in plane]
-    diagonal = [
-        {"sx": at(n_x, sx, dx), "sy": at(n_y, sy, dy)} for dx in (-1, 1) for dy in (-1, 1)
-    ]
     beside = {"sy": at(n_y, sy, 2 * core - 1)}
 
     barrier = pltpu.get_barrier_semaphore()
     near_x = [{"sx": at(n_x, sx, k)} for k in (-1, 1)]
     near_y = [{"sy": at(n_y, sy, k)} for k in (-2, 2)]
     near_b = [{"batch": at(n_b, sb, k)} for k in (-1, 1)]
-    greeted = near_x + diagonal + [beside, sibling] + near_y + near_b
+    greeted = near_x + [beside, sibling] + near_y + near_b
     for device in greeted:
         pl.semaphore_signal(barrier, inc=1, device_id=device, device_id_type=MESH)
 
@@ -146,27 +145,9 @@
         sends.append(cp)
         return cp
 
-    def piece(q):
-        start = 1 if q == 0 else 2 * LAST[q - 1] + 2
-        stop = min(2 * LAST[q] + 2, BY + 1)
-        return pl.ds(start, stop - start)
-
-    ccopies = []
-    for d, (src_x, dst_x) in enumerate(((1, BX + 1), (BX, 0))):
-        for f, (src_y, dst_y) in enumerate(((1, BY + 1), (BY, 0))):
-            ccopies.append(
-                send(
-                    cells.at[src_x, src_y],
-                    cells.at[dst_x, dst_y],
-                    cs_send.at[2 * d + f],
-                    cs_recv.at[2 * d + f],
-                    {"sx": at(n_x, sx, 2 * d - 1), "sy": at(n_y, sy, 2 * f - 1)},
-                )
-            )
-
     xcopies = []
-    for q in range(len(LAST)):
-        rows = piece(q)
+    for q, (start, size) in enumerate(PIECES):
+        rows = pl.ds(start, size)
         for d, (src_x, dst_x) in enumerate(((1, BX + 1), (BX, 0))):
             xcopies.append(
                 send(
@@ -272,6 +253,29 @@
 
     x_first, x_last = sx == 0, sx == n_x - 1
     y_first, y_last = sy == 0, sy == n_y - 1
+    def arrive(q):
+        start, size = PIECES[q]
+        xcopies[2 * q].wait_recv()
+        clear(x_last, BX + 1, start, 1, size)
+        xcopies[2 * q + 1].wait_recv()
+        clear(x_first, 0, start, 1, size)
+
+    arrive(0)
+    arrive(1)
+    ccopies = []
+    for d, x in enumerate((BX + 1, 0)):
+        for f, (src_y, dst_y) in enumerate(((1, BY + 1), (BY, 0))):
+            ccopies.append(
+                send(
+                    cells.at[x, src_y],
+                    cells.at[x, dst_y],
+                    cs_send.at[2 * d + f],
+                    cs_recv.at[2 * d + f],
+                    {"sy": at(n_y, sy, 2 * f - 1)},
+                )
+            )
+
+
     ycopies[0].wait_recv()
     clear(y_last, 1, BY + 1, BX, 1)
     ycopies[1].wait_recv()
@@ -285,15 +289,14 @@
             clear(jnp.logical_or(x_edge, y_edge), x, y, 1, 1)
 
     hear(2)
-    corner(1, 0, y_first)
-    corner(0, BY + 1, y_last)
-    for q in range(len(LAST)):
-        rows = piece(q)
-        xcopies[2 * q].wait_recv()
-        clear(x_last, BX + 1, rows.start, 1, rows.size)
-        xcopies[2 * q + 1].wait_recv()
-        clear(x_first, 0, rows.start, 1, rows.size)
-        several(1, LAST[q - 1] if q else 0, LAST[q])
+    for q in range(2, len(PIECES)):
+        arrive(q)
+        for p in READY[q]:
+            if p == 0:
+                corner(1, 0, y_first)
+            elif p == 7:
+                corner(0, BY + 1, y_last)
+            one(1, p)
 
     def turned(col):
         return jnp.sum(eye2 * col, axis=0, keepdims=True)
@@ -330,9 +333,10 @@
         ]
         for cp in copies:
             cp.wait_recv()
-        total = moved[0]
-        for i in range(1, n):
-            total = total + moved[i]
+        parts = [moved[i] for i in range(n)]
+        while len(parts) > 1:
+            parts = [u + v for u, v in zip(parts[::2], parts[1::2])]
+        total = parts[0]
         means = total[16:]
         line = jnp.sum(means, axis=0, keepdims=True)
         mean = jnp.where(lane1 < C, line * (1.0 / n), 0.0)
@@ -352,11 +356,11 @@
     count = float(LOCAL)
     state = merge(products, diag, mean, count, 2, core, [sibling], moved_c, rc_send, rc_recv)
     count *= 2
-    state = merge(
+    state = merge(*state, count, n_x, sx, others_x, moved_x, rx_send, rx_recv)
+    count *= n_x
+    products, diag, mean = merge(
         *state, count, n_chip * n_b, chip * n_b + sb, others_p, moved_p, rp_send, rp_recv
     )
-    count *= n_chip * n_b
-    products, diag, mean = merge(*state, count, n_x, sx, others_x, moved_x, rx_send, rx_recv)
 
     half = jnp.concatenate([products, pltpu.roll(products, C, 1)], axis=0)
     across = jnp.concatenate([half, jnp.zeros((128 - H, 128), F32)], axis=0).T
@@ -437,8 +441,8 @@
             dma((4,)),
             dma,
             dma((2,)),
-            dma((2 * len(LAST),)),
-            dma((2 * len(LAST),)),
+            dma((2 * len(PIECES),)),
+            dma((2 * len(PIECES),)),
             dma((2,)),
             dma((2,)),
             dma((4,)),

time: 36.3 us -> 35.9 us (0.989)
  Pallas kernels: 36.2 us -> 35.8 us
    pallas_call x1, Pallas kernels: 34.8 us -> 34.3 us  [on_device(): pl.pallas_call(lambda *refs: body((n_x, n_y, n_b), *refs), out_shape=[jax...]
where the time goes in v5:
time: 35.9 us; the launch traced here: 35.8 us
  Pallas kernels  35.8 us (100%)
    pallas_call x1, Pallas kernels, on_device(): pl.pallas_call(lambda *refs: body((n_x, n_y, n_b), *refs), out_shape=[jax...  34.3 us
    pallas_call x1, Pallas kernels, on_device(): pl.pallas_call(mix_body, out_shape=jax.ShapeDtypeStruct((C, BX * BY, NZ),...  1.49 us

profile of v5, /device:TPU:1, one launch (start us, length us, event | category | flops | bytes accessed | tf_op | source)
XLA Modules:
  0.0 35.8 jit_solution(10554924035898072797)
XLA Ops:
  0.0 34.3 %shard_map.46 = (bf16[16,128,512]{2,1,0:T(8,128)(2,1)S(1)}, bf16[64,192]{1,0:T(8,128)(2,1)S(1)}, f32[64,128]{1,0:T(8,128)S(1)}) custom-call(bf16[1,64,4,16,128]{4,3,2,1,0:T(8,128)(2,1)} %refs_0_.1, bf16[27,64,64]{2,1,0:T(8,128)(2,1)} %bitcast.6, f32[1,64]{1,0:T(1,128)} %bitcast.7, f32[1,64]{1,0:T(1,128)} %bitcast.8), custom_call_target="tpu_custom_call" | custom-call | tf_op jit(solution)/shard_map/pallas_call | solution.py:419
  34.3 1.5 %shard_map.47 = f32[64,64,128]{2,1,0:T(8,128)} custom-call(bf16[16,128,512]{2,1,0:T(8,128)(2,1)S(1)} %get-tuple-element.8.held, bf16[64,192]{1,0:T(8,128)(2,1)S(1)} %get-tuple-element.9.mixer, f32[64,128]{1,0:T(8,128)S(1)} %get-tuple-element.10.offset), custom_call_target="tpu_custom_call" | custom-call | tf_op jit(solution)/shard_map/pallas_call | solution.py:462

commit v6 on v5

--- a/solution.py
+++ b/solution.py
@@ -322,22 +322,25 @@
     lane1 = lane[:1]
 
     def merge(products, diag, mean, count, n, me, others, moved, s_sem, r_sem):
-        high = moved.shape[1] - 16
+        high = 8 if n <= 8 else 16
         rows = row[:high]
         line = jnp.where(lane1 < C, mean, jnp.where(lane1 < C + H, diag, 0.0))
         moved[me, pl.ds(0, 16)] = products
-        moved[me, pl.ds(16, high)] = jnp.where(rows == me, line, 0.0)
+        moved[me, pl.ds(16, 1)] = line
+        used = moved.at[me, pl.ds(0, 17)]
         copies = [
-            send(moved.at[me], moved.at[me], s_sem.at[k], r_sem.at[k], device)
+            send(used, used, s_sem.at[k], r_sem.at[k], device)
             for k, device in enumerate(others)
         ]
         for cp in copies:
             cp.wait_recv()
-        parts = [moved[i] for i in range(n)]
-        while len(parts) > 1:
-            parts = [u + v for u, v in zip(parts[::2], parts[1::2])]
-        total = parts[0]
-        means = total[16:]
+        def tree(parts):
+            while len(parts) > 1:
+                parts = [u + v for u, v in zip(parts[::2], parts[1::2])]
+            return parts[0]
+
+        total = tree([moved[i, pl.ds(0, 16)] for i in range(n)])
+        means = tree([jnp.where(rows == i, moved[i, pl.ds(16, 1)], 0.0) for i in range(n)])
         line = jnp.sum(means, axis=0, keepdims=True)
         mean = jnp.where(lane1 < C, line * (1.0 / n), 0.0)
         off = jnp.where(jnp.logical_and(rows < n, lane[:high] < C), means - mean, 0.0)
@@ -351,7 +354,7 @@
             preferred_element_type=F32,
         )
         more, more_diag = pack(outer[:C])
-        return total[:16] + count * more, line + count * more_diag, mean + pltpu.roll(mean, C, 1)
+        return total + count * more, line + count * more_diag, mean + pltpu.roll(mean, C, 1)
 
     count = float(LOCAL)
     state = merge(products, diag, mean, count, 2, core, [sibling], moved_c, rc_send, rc_recv)
@@ -435,7 +438,7 @@
             pltpu.VMEM((C, 128), F32),
             pltpu.VMEM((C, 128), F32),
             pltpu.VMEM((2, 24, 128), F32),
-            pltpu.VMEM((n_p, 32, 128), F32),
+            pltpu.VMEM((n_p, 24, 128), F32),
             pltpu.VMEM((n_x, 24, 128), F32),
             pltpu.VMEM((2, C), F32),
             dma((4,)),

time: 35.9 us -> 34.7 us (0.967)
  Pallas kernels: 35.8 us -> 34.6 us
    pallas_call x1, Pallas kernels: 34.3 us -> 33.1 us  [on_device(): pl.pallas_call(lambda *refs: body((n_x, n_y, n_b), *refs), out_shape=[jax...]
where the time goes in v6:
time: 34.7 us; the launch traced here: 34.6 us
  Pallas kernels  34.6 us (100%)
    pallas_call x1, Pallas kernels, on_device(): pl.pallas_call(lambda *refs: body((n_x, n_y, n_b), *refs), out_shape=[jax...  33.1 us
    pallas_call x1, Pallas kernels, on_device(): pl.pallas_call(mix_body, out_shape=jax.ShapeDtypeStruct((C, BX * BY, NZ),...  1.49 us

profile of v6, /device:TPU:1, one launch (start us, length us, event | category | flops | bytes accessed | tf_op | source)
XLA Modules:
  0.0 34.6 jit_solution(10294601335704522751)
XLA Ops:
  0.0 33.1 %shard_map.46 = (bf16[16,128,512]{2,1,0:T(8,128)(2,1)S(1)}, bf16[64,192]{1,0:T(8,128)(2,1)S(1)}, f32[64,128]{1,0:T(8,128)S(1)}) custom-call(bf16[1,64,4,16,128]{4,3,2,1,0:T(8,128)(2,1)} %refs_0_.1, bf16[27,64,64]{2,1,0:T(8,128)(2,1)} %bitcast.6, f32[1,64]{1,0:T(1,128)} %bitcast.7, f32[1,64]{1,0:T(1,128)} %bitcast.8), custom_call_target="tpu_custom_call" | custom-call | tf_op jit(solution)/shard_map/pallas_call | solution.py:422
  33.1 1.5 %shard_map.47 = f32[64,64,128]{2,1,0:T(8,128)} custom-call(bf16[16,128,512]{2,1,0:T(8,128)(2,1)S(1)} %get-tuple-element.8.held, bf16[64,192]{1,0:T(8,128)(2,1)S(1)} %get-tuple-element.9.mixer, f32[64,128]{1,0:T(8,128)S(1)} %get-tuple-element.10.offset), custom_call_target="tpu_custom_call" | custom-call | tf_op jit(solution)/shard_map/pallas_call | solution.py:465

commit v7 on v6

--- a/solution.py
+++ b/solution.py
@@ -82,6 +82,26 @@
     def at(n, i, k):
         return lax.rem(i + (k + n), n)
 
+    n_chip = n_y // 2
+    core = lax.rem(sy, 2)
+    chip = sy // 2
+    sibling = {"sy": sy + (1 - 2 * core)}
+    others_x = [{"sx": at(n_x, sx, k)} for k in sorted(range(1, n_x), key=lambda k: -min(k, n_x - k))]
+    plane = sorted(
+        ((j, k) for j in range(n_chip) for k in range(n_b) if j or k),
+        key=lambda o: -min(o[0], n_chip - o[0]) - min(o[1], n_b - o[1]),
+    )
+    others_p = [{"sy": 2 * at(n_chip, chip, j) + core, "batch": at(n_b, sb, k)} for j, k in plane]
+    beside = {"sy": at(n_y, sy, 2 * core - 1)}
+
+    barrier = pltpu.get_barrier_semaphore()
+    near_x = [{"sx": at(n_x, sx, k)} for k in (-1, 1)]
+    near_y = [{"sy": at(n_y, sy, k)} for k in (-2, 2)]
+    near_b = [{"batch": at(n_b, sb, k)} for k in (-1, 1)]
+    greeted = near_x + [beside, sibling] + near_y + near_b
+    for device in greeted:
+        pl.semaphore_signal(barrier, inc=1, device_id=device, device_id_type=MESH)
+
     loads = []
     for k, x in enumerate((0, 3, 1, 2)):
         cp = pltpu.make_async_copy(vol.at[0, :, x], vin.at[x], load_sem.at[k])
@@ -93,26 +113,6 @@
     gcp.start()
     hcp = pltpu.make_async_copy(shift, vec.at[pl.ds(1, 1)], vsem.at[1])
     hcp.start()
-
-    n_chip = n_y // 2
-    core = lax.rem(sy, 2)
-    chip = sy // 2
-    sibling = {"sy": sy + (1 - 2 * core)}
-    others_x = [{"sx": at(n_x, sx, k)} for k in sorted(range(1, n_x), key=lambda k: -min(k, n_x - k))]
-    plane = sorted(
-        ((j, k) for j in range(n_chip) for k in range(n_b) if j or k),
-        key=lambda o: -min(o[0], n_chip - o[0]) - min(o[1], n_b - o[1]),
-    )
-    others_p = [{"sy": 2 * at(n_chip, chip, j) + core, "batch": at(n_b, sb, k)} for j, k in plane]
-    beside = {"sy": at(n_y, sy, 2 * core - 1)}
-
-    barrier = pltpu.get_barrier_semaphore()
-    near_x = [{"sx": at(n_x, sx, k)} for k in (-1, 1)]
-    near_y = [{"sy": at(n_y, sy, k)} for k in (-2, 2)]
-    near_b = [{"batch": at(n_b, sb, k)} for k in (-1, 1)]
-    greeted = near_x + [beside, sibling] + near_y + near_b
-    for device in greeted:
-        pl.semaphore_signal(barrier, inc=1, device_id=device, device_id_type=MESH)
 
     def tell(k):
         for device in near_x:

time: 34.7 us -> 34.7 us (level)
  no operation moved by 1% of the time
where the time goes in v7:
time: 34.7 us; the launch traced here: 34.6 us
  Pallas kernels  34.6 us (100%)
    pallas_call x1, Pallas kernels, on_device(): pl.pallas_call(lambda *refs: body((n_x, n_y, n_b), *refs), out_shape=[jax...  33.1 us
    pallas_call x1, Pallas kernels, on_device(): pl.pallas_call(mix_body, out_shape=jax.ShapeDtypeStruct((C, BX * BY, NZ),...  1.49 us

profile of v7, /device:TPU:1, one launch (start us, length us, event | category | flops | bytes accessed | tf_op | source)
XLA Modules:
  0.0 34.6 jit_solution(17448194476573430496)
XLA Ops:
  0.0 33.1 %shard_map.46 = (bf16[16,128,512]{2,1,0:T(8,128)(2,1)S(1)}, bf16[64,192]{1,0:T(8,128)(2,1)S(1)}, f32[64,128]{1,0:T(8,128)S(1)}) custom-call(bf16[1,64,4,16,128]{4,3,2,1,0:T(8,128)(2,1)} %refs_0_.1, bf16[27,64,64]{2,1,0:T(8,128)(2,1)} %bitcast.6, f32[1,64]{1,0:T(1,128)} %bitcast.7, f32[1,64]{1,0:T(1,128)} %bitcast.8), custom_call_target="tpu_custom_call" | custom-call | tf_op jit(solution)/shard_map/pallas_call | solution.py:422
  33.1 1.5 %shard_map.47 = f32[64,64,128]{2,1,0:T(8,128)} custom-call(bf16[16,128,512]{2,1,0:T(8,128)(2,1)S(1)} %get-tuple-element.8.held, bf16[64,192]{1,0:T(8,128)(2,1)S(1)} %get-tuple-element.9.mixer, f32[64,128]{1,0:T(8,128)S(1)} %get-tuple-element.10.offset), custom_call_target="tpu_custom_call" | custom-call | tf_op jit(solution)/shard_map/pallas_call | solution.py:465
